TPU v7x, 256 devices: a whole 4x4x8 slice. The times are simulated.
256 devices in a mesh: dp: 32 (over z_lo, x, core), tp: 8 (over z_hi, y).
Axes of the slice: x: 4, y: 4, z: 8 (z_hi: 2, z_lo: 4; z = z_hi * 4 + z_lo), core: 2. Of those that a mesh axis runs over, the one named last changes fastest.
Arguments:
- tokens: bfloat16 [6144, 3584], P('dp', 'tp'), may hold values from -6 to 6
- cotangent: bfloat16 [6144, 3584], P('dp', 'tp'), may hold values from -6 to 6
- working: bfloat16 [32, 8, 3, 384, 3584], P('dp', 'tp'), may hold values from -0.09375 to 0.09375
- degraded: int32 [32], P('dp'), may hold values from 0 to 1, as said below
- block_map: int32 [32, 16], P('dp'), may hold values from 0 to 7, as said below
- master: float32 [3, 2048, 3584], P(None, ('tp', 'dp')), may hold values from -6 to 6
- moment_one: float32 [3, 2048, 3584], P(None, ('tp', 'dp')), may hold values from -6 to 6
- moment_two: float32 [3, 2048, 3584], P(None, ('tp', 'dp')), may hold values from 0.5 to 8
Outputs:
- input_grad: bfloat16 [6144, 3584], P('dp', 'tp')
- master_next: float32 [3, 2048, 3584], P(None, ('tp', 'dp'))
- moment_one_next: float32 [3, 2048, 3584], P(None, ('tp', 'dp'))
- moment_two_next: float32 [3, 2048, 3584], P(None, ('tp', 'dp'))
Inputs may be any that keep to these rules, and one draw needn't show every extreme that they name: `degraded`: exactly 8 replicas have the value 1. `block_map`: in every row the 16 blocks lie on 6 distinct devices, each of which holds 2 or 3 of them, and at least one holds 3. A row is read only where degraded is 1.
All inputs are finite; a program needn't handle non-finite values.
Results may differ from a plain program's by a relative error of at most 0.0075.
Values may be sent and summed in bfloat16 or wider, within the bound.
A program may use at most 64 MiB of HBM per device.

v0:
```python
import jax
import jax.numpy as jnp
from jax import lax
from jax.sharding import PartitionSpec as P

BLOCK = 128
BLOCKS = 16
beta_one = 0.9
beta_two = 0.95
learn_rate = 0.05
decay_rate = 0.1
adam_eps = 1e-08
bias_one = 1.0 - 0.9**10
bias_two = 1.0 - 0.95**10


def layout_places(replica_flag, mapping, tp_size, slot_count):
    blocks = jnp.arange(BLOCKS, dtype=jnp.int32)
    canonical = blocks // (BLOCKS // tp_size)
    holder = jnp.where(replica_flag > 0, mapping, canonical)
    earlier = (holder[None, :] == holder[:, None]) & (blocks[None, :] < blocks[:, None])
    slot_rank = jnp.sum(earlier.astype(jnp.int32), axis=1)
    return holder * slot_count + slot_rank


def per_device(tokens, cotangent, working, degraded, block_map, master, moment_one, moment_two):
    tp_size = lax.axis_size("tp")
    replicas = lax.axis_size("dp")
    my_index = lax.axis_index("tp")
    weights = working[0, 0]
    slot_count = weights.shape[1] // BLOCK
    per_dev = BLOCKS // tp_size
    places = layout_places(degraded[0], block_map[0], tp_size, slot_count)
    my_slots = my_index * slot_count + jnp.arange(slot_count, dtype=jnp.int32)
    holding = places[:, None] == my_slots[None, :]
    filled = jnp.any(holding, axis=0).astype(jnp.float32)
    column_mask = jnp.repeat(filled, BLOCK)
    inputs, upstream = (
        lax.all_gather(tokens, "tp", axis=1, tiled=True),
        lax.all_gather(cotangent, "tp", axis=1, tiled=True),
    )
    contract_d = (((1,), (1,)), ((), ()))
    gate_pre = lax.dot_general(inputs, weights[0], contract_d, preferred_element_type=jnp.float32)
    up_pre = lax.dot_general(inputs, weights[1], contract_d, preferred_element_type=jnp.float32)
    hidden_grad = lax.dot_general(
        upstream, weights[2], contract_d, preferred_element_type=jnp.float32
    )
    gate_sig = jax.nn.sigmoid(gate_pre)
    active = gate_pre * gate_sig
    hidden = (active * up_pre * column_mask).astype(jnp.bfloat16)
    gate_grad = (
        hidden_grad * up_pre * gate_sig * (1.0 + gate_pre * (1.0 - gate_sig)) * column_mask
    ).astype(jnp.bfloat16)
    up_grad = (hidden_grad * active * column_mask).astype(jnp.bfloat16)
    partial_value = jnp.dot(gate_grad, weights[0], preferred_element_type=jnp.float32) + jnp.dot(
        up_grad, weights[1], preferred_element_type=jnp.float32
    )
    input_grad = lax.psum_scatter(partial_value, "tp", scatter_dimension=1, tiled=True).astype(
        jnp.bfloat16
    )
    tok_rows = gate_grad.shape[0]
    packed = jnp.stack(
        [
            hidden.reshape(tok_rows, slot_count, BLOCK),
            gate_grad.reshape(tok_rows, slot_count, BLOCK),
            up_grad.reshape(tok_rows, slot_count, BLOCK),
        ],
        axis=2,
    )
    packed = packed.transpose(1, 0, 2, 3).reshape(slot_count, tok_rows, 3 * BLOCK)
    wanted = lax.dynamic_slice_in_dim(places, my_index * per_dev, per_dev)
    shard_piece = lax.all_gather(packed, "tp", axis=0, tiled=True)
    positions = jnp.arange(shard_piece.shape[0], dtype=jnp.int32)
    selector = (wanted[:, None] == positions[None, :]).astype(jnp.bfloat16)
    owned_acts = jnp.einsum(
        "kn,ntc->ktc", selector, shard_piece, preferred_element_type=jnp.float32
    ).astype(jnp.bfloat16)
    owned_kinds = (
        owned_acts.reshape(per_dev, tok_rows, 3, BLOCK)
        .transpose(2, 1, 0, 3)
        .reshape(3, tok_rows, per_dev * BLOCK)
    )
    contract_t = (((0,), (0,)), ((), ()))
    gate_term = lax.dot_general(
        owned_kinds[1], inputs, contract_t, preferred_element_type=jnp.float32
    )
    up_term = lax.dot_general(
        owned_kinds[2], inputs, contract_t, preferred_element_type=jnp.float32
    )
    down_term = lax.dot_general(
        owned_kinds[0], upstream, contract_t, preferred_element_type=jnp.float32
    )
    summed = lax.psum_scatter(
        jnp.stack([gate_term, up_term, down_term], axis=1).astype(jnp.bfloat16),
        "dp",
        scatter_dimension=0,
        tiled=True,
    ).astype(jnp.float32)
    grad_mean = jnp.transpose(summed, (1, 0, 2)) / replicas
    moment_one_next = beta_one * moment_one + (1.0 - beta_one) * grad_mean
    moment_two_next = beta_two * moment_two + (1.0 - beta_two) * grad_mean * grad_mean
    update = (
        moment_one_next / bias_one / (jnp.sqrt(moment_two_next / bias_two) + adam_eps)
        + decay_rate * master
    )
    master_next = master - learn_rate * update
    return (input_grad, master_next, moment_one_next, moment_two_next)


def solution(mesh):
    return jax.shard_map(
        per_device,
        mesh=mesh,
        in_specs=(
            P("dp", "tp"),
            P("dp", "tp"),
            P("dp", "tp", None, None, None),
            P("dp"),
            P("dp", None),
            P(None, ("tp", "dp"), None),
            P(None, ("tp", "dp"), None),
            P(None, ("tp", "dp"), None),
        ),
        out_specs=(
            P("dp", "tp"),
            P(None, ("tp", "dp"), None),
            P(None, ("tp", "dp"), None),
            P(None, ("tp", "dp"), None),
        ),
        check_vma=False,
    )
```

profile of v0, /device:TPU:24, one launch (start us, length us, event | category | flops | bytes accessed | tf_op | source)
XLA Modules:
  0.0 538.7 jit_solution(16597101864245584908)
XLA Ops:
  7.2 0.7 all-gather.10.cloned.1.call-update
  7.9 0.7 all-gather.8.cloned.1.call-update
  9.4 0.7 broadcast_select_fusion.1
  10.2 0.7 multiply_add_fusion
  11.2 71.0 %all-gather.10.cloned.1.call-done = bf16[8,448,192]{1,2,0:T(8,128)(2,1)} async-done(((bf16[1,448,192]{1,2,0:T(8,128)(2,1)}), bf16[8,448,192]{1,2,0:T(8,128)(2,1)}) %all-gather.10.cloned.1.call-update) | async-done | bytes 1376272 | tf_op jit(solution)/shard_map/all_gather | solution.py:39
  82.2 2.3 copy.30
  84.5 1.8 reshape.101
  86.3 63.5 %all-gather.8.cloned.1.call-done = bf16[8,448,192]{1,2,0:T(8,128)(2,1)} async-done(((bf16[1,448,192]{1,2,0:T(8,128)(2,1)}), bf16[8,448,192]{1,2,0:T(8,128)(2,1)}) %all-gather.8.cloned.1.call-update) | async-done | bytes 1376272 | tf_op jit(solution)/shard_map/all_gather | solution.py:40
  149.8 2.3 copy.29
  152.1 2.7 reshape.99
  154.8 2.9 fusion.7
  157.7 2.8 fusion.12
  160.5 3.6 multiply_convert_fusion
  164.2 0.6 copy-done.1
  164.8 1.0 stack_reshape.9
  165.8 0.5 maximum_bitcast_fusion.1
  166.3 0.5 copy.31
  166.8 1.2 reshape.96
  168.0 2.7 fusion.5
  170.7 4.2 convolution_add_fusion
  174.9 4.8 copy.37
  180.1 80.5 %all-gather.6.cloned.1.call-done = bf16[24,192,384]{2,1,0:T(8,128)(2,1)} async-done(((bf16[3,192,384]{2,1,0:T(8,128)(2,1)}), bf16[24,192,384]{2,1,0:T(8,128)(2,1)}) %all-gather.6.cloned.1.call-update) | async-done | bytes 3538960 | tf_op jit(solution)/shard_map/all_gather | solution.py:72
  260.6 4.6 fusion.19
  266.2 0.7 fusion.2
  266.9 0.7 fusion.1
  267.6 0.7 fusion
  268.2 0.7 maximum_bitcast_fusion
  269.0 2.8 copy.41
  271.8 107.1 %reduce-scatter.7.cloned.1.call-done = f32[448,192]{1,0:T(8,128)} async-done(((f32[3584,192]{1,0:T(8,128)}), f32[448,192]{1,0:T(8,128)}) %reduce-scatter.7.cloned.1.call-update) | async-done | bytes 344080
  378.9 1.8 copy.38
  380.7 149.4 %reduce-scatter.9.cloned.1.call-done = bf16[8,10752]{1,0:T(8,128)(2,1)} async-done(((bf16[256,10752]{1,0:T(8,128)(2,1)}), bf16[8,10752]{1,0:T(8,128)(2,1)}) %reduce-scatter.9.cloned.1.call-update) | async-done | bytes 172048
  530.1 2.0 multiply_subtract_fusion
  (34 shorter events, 2.1 us)
Async XLA Ops:
  7.2 75.0 %all-gather.10.cloned.1.call-start = ((), (), s32[]{:S(2)}) async-start(), calls=%async_computation.4 | async-start | bytes 1769472 | tf_op jit(solution)/shard_map/all_gather | solution.py:39
  7.9 141.9 %all-gather.8.cloned.1.call-start = ((), (), s32[]{:S(2)}) async-start(), calls=%async_computation.3 | async-start | bytes 1769472 | tf_op jit(solution)/shard_map/all_gather | solution.py:40
  8.6 251.9 %all-gather.6.cloned.1.call-start = ((), (), s32[]{:S(2)}) async-start(), calls=%async_computation.2 | async-start | bytes 3981312 | tf_op jit(solution)/shard_map/all_gather | solution.py:72
  154.8 2.9 copy-start
  164.1 0.7 copy-start.1
  167.9 2.7 copy-start.2
  168.0 210.9 %reduce-scatter.7.cloned.1.call-start = ((), (), s32[]{:S(2)}) async-start(), calls=%async_computation.5 | async-start | bytes 4128768
  179.8 350.3 %reduce-scatter.9.cloned.1.call-start = ((), (), s32[]{:S(2)}) async-start(), calls=%async_computation.6 | async-start | bytes 5677056
  271.8 258.3 %copy-start.3 = (f32[3,8,3584]{2,1,0:T(8,128)S(1)}, f32[3,8,3584]{2,1,0:T(8,128)}, u32[]{:S(2)}) copy-start(f32[3,8,3584]{2,1,0:T(8,128)} %param.13) | copy-start | bytes 1032196
  271.8 258.3 %copy-start.4 = (f32[3,8,3584]{2,1,0:T(8,128)S(1)}, f32[3,8,3584]{2,1,0:T(8,128)}, u32[]{:S(2)}) copy-start(f32[3,8,3584]{2,1,0:T(8,128)} %param.14) | copy-start | bytes 1032196
  271.8 258.3 %copy-start.5 = (f32[3,8,3584]{2,1,0:T(8,128)S(1)}, f32[3,8,3584]{2,1,0:T(8,128)}, u32[]{:S(2)}) copy-start(f32[3,8,3584]{2,1,0:T(8,128)} %param.15) | copy-start | bytes 1032196
Sparse Core Ops, SparseCore 0:
  10.6 71.5 all-gather.9
  84.8 64.9 all-gather.7
  168.1 92.4 all-gather.5
  264.7 114.1 reduce-scatter.6
  381.4 148.5 reduce-scatter.8
where the time goes:
time: 539 us
  waiting for transfers between devices  473 us (88%)
  local copies, waits for them, and re-layouts  22.9 us (4%)
  matrix products  22.8 us (4%)
  between operations  14.6 us (3%)
    unnamed x7, waiting for transfers between devices  258 us
    all_gather x1, waiting for transfers between devices, per_device(): shard_piece = lax.all_gather(packed, 'tp', axis=0, tiled=True)  80.5 us
    all_gather x1, waiting for transfers between devices, per_device(): lax.all_gather(tokens, 'tp', axis=1, tiled=True)  71 us
    all_gather x1, waiting for transfers between devices, per_device(): lax.all_gather(cotangent, 'tp', axis=1, tiled=True)  63.5 us
    unnamed x17, local copies, waits for them, and re-layouts  14.5 us
  transfers between devices with their start and end apart: 5, of which 5 were waited for; matrix products, arithmetic and copies ran while one was open for 6% of the time, Pallas kernels for 0%

commit v1 on v0

--- a/solution.py
+++ b/solution.py
@@ -36,7 +36,9 @@
     filled = jnp.any(holding, axis=0).astype(jnp.float32)
     column_mask = jnp.repeat(filled, BLOCK)
     inputs, upstream = (
-        lax.all_gather(tokens, "tp", axis=1, tiled=True),
+        jnp.concatenate(
+            lax.all_to_all(jnp.stack([tokens] * lax.axis_size("tp")), "tp", 0, 0), axis=1
+        ),
         lax.all_gather(cotangent, "tp", axis=1, tiled=True),
     )
     contract_d = (((1,), (1,)), ((), ()))

time: 539 us -> 493 us (0.915)
  waiting for transfers between devices: 473 us -> 416 us
  starting transfers between devices: 0.38 us -> 11.6 us
    all_gather x1 -> x0, waiting for transfers between devices: 71 us -> none  [per_device(): lax.all_gather(tokens, 'tp', axis=1, tiled=True)]
    all_to_all x0 -> x1, waiting for transfers between devices: none -> 27.7 us  [per_device(): lax.all_to_all(jnp.stack([tokens] * lax.axis_size('tp')), 'tp', 0, 0)]
    all_gather x1, waiting for transfers between devices: 63.5 us -> 51.1 us  [per_device(): lax.all_gather(cotangent, 'tp', axis=1, tiled=True)]
    all_to_all x0 -> x1, starting transfers between devices: none -> 11.3 us  [per_device(): lax.all_to_all(jnp.stack([tokens] * lax.axis_size('tp')), 'tp', 0, 0)]
    unnamed x17 -> x18, local copies, waits for them, and re-layouts: 14.5 us -> 12.7 us
    unnamed x7 -> x6, waiting for transfers between devices: 258 us -> 257 us
where the time goes in v1:
time: 493 us
  waiting for transfers between devices  416 us (84%)
  local copies, waits for them, and re-layouts  23.7 us (5%)
  matrix products  22.8 us (5%)
  between operations  14.6 us (3%)
  starting transfers between devices  11.6 us (2%)
    unnamed x6, waiting for transfers between devices  257 us
    all_gather x1, waiting for transfers between devices, per_device(): shard_piece = lax.all_gather(packed, 'tp', axis=0, tiled=True)  80.5 us
    all_gather x1, waiting for transfers between devices, per_device(): lax.all_gather(cotangent, 'tp', axis=1, tiled=True)  51.1 us
    all_to_all x1, waiting for transfers between devices, per_device(): lax.all_to_all(jnp.stack([tokens] * lax.axis_size('tp')), 'tp', 0, 0)  27.7 us
    unnamed x18, local copies, waits for them, and re-layouts  12.7 us
    all_to_all x1, starting transfers between devices, per_device(): lax.all_to_all(jnp.stack([tokens] * lax.axis_size('tp')), 'tp', 0, 0)  11.3 us
  transfers between devices with their start and end apart: 5, of which 5 were waited for; matrix products, arithmetic and copies ran while one was open for 6% of the time, Pallas kernels for 0%

profile of v1, /device:TPU:24, one launch (start us, length us, event | category | flops | bytes accessed | tf_op | source)
XLA Modules:
  0.0 492.9 jit_solution(7930840731881694501)
XLA Ops:
  7.2 2.2 stack.30
  9.4 11.3 %all-to-all-start = ((bf16[8,192,448]{2,1,0:T(8,128)(2,1)}), bf16[8,192,448]{2,1,0:T(8,128)(2,1)S(1)}, u32[]{:S(2)}, u32[]{:S(2)}) async-start(bf16[8,192,448]{2,1,0:T(8,128)(2,1)} %stack.30), calls=%async_computation | async-start | bytes 3145728 | tf_op jit(solution)/shard_map/all_to_all | solution.py:40
  20.7 0.7 all-gather.6.cloned.1.call-update
  22.6 27.7 %all-to-all-done = bf16[8,192,448]{2,1,0:T(8,128)(2,1)S(1)} async-done(((bf16[8,192,448]{2,1,0:T(8,128)(2,1)}), bf16[8,192,448]{2,1,0:T(8,128)(2,1)S(1)}, u32[]{:S(2)}, u32[]{:S(2)}) %all-to-all-start) | async-done | bytes 1376288 | tf_op jit(solution)/shard_map/all_to_all | solution.py:40
  50.4 0.9 copy.29
  51.3 1.8 reshape.105
  53.1 51.1 %all-gather.6.cloned.1.call-done = bf16[8,448,192]{1,2,0:T(8,128)(2,1)} async-done(((bf16[1,448,192]{1,2,0:T(8,128)(2,1)}), bf16[8,448,192]{1,2,0:T(8,128)(2,1)}) %all-gather.6.cloned.1.call-update) | async-done | bytes 1376272 | tf_op jit(solution)/shard_map/all_gather | solution.py:42
  104.2 2.3 copy.28
  106.4 2.7 reshape.109
  109.1 2.9 fusion.7
  112.1 2.8 fusion.12
  114.9 3.6 multiply_convert_fusion
  118.5 0.6 copy-done.1
  119.2 1.0 stack_reshape.9
  120.2 0.5 maximum_bitcast_fusion.1
  120.6 0.5 copy.30
  121.1 1.2 reshape.106
  122.4 2.7 fusion.5
  125.0 4.2 convolution_add_fusion
  129.2 4.8 copy.36
  134.4 80.5 %all-gather.4.cloned.1.call-done = bf16[24,192,384]{2,1,0:T(8,128)(2,1)} async-done(((bf16[3,192,384]{2,1,0:T(8,128)(2,1)}), bf16[24,192,384]{2,1,0:T(8,128)(2,1)}) %all-gather.4.cloned.1.call-update) | async-done | bytes 3538960 | tf_op jit(solution)/shard_map/all_gather | solution.py:74
  214.9 4.6 fusion.19
  219.7 0.4 fusion.42
  220.6 0.7 fusion.2
  221.3 0.7 fusion.1
  221.9 0.7 fusion
  222.6 0.7 maximum_bitcast_fusion
  223.3 2.8 copy.40
  226.1 106.9 %reduce-scatter.7.cloned.1.call-done = f32[448,192]{1,0:T(8,128)} async-done(((f32[3584,192]{1,0:T(8,128)}), f32[448,192]{1,0:T(8,128)}) %reduce-scatter.7.cloned.1.call-update) | async-done | bytes 344080
  333.1 1.8 copy.37
  334.9 149.4 %reduce-scatter.9.cloned.1.call-done = bf16[8,10752]{1,0:T(8,128)(2,1)} async-done(((bf16[256,10752]{1,0:T(8,128)(2,1)}), bf16[8,10752]{1,0:T(8,128)(2,1)}) %reduce-scatter.9.cloned.1.call-update) | async-done | bytes 172048
  484.3 2.0 multiply_subtract_fusion
  (36 shorter events, 1.6 us)
Async XLA Ops:
  7.2 15.0 %copy-start.6 = (s32[1,16]{1,0:T(1,128)S(1)}, s32[1,16]{1,0:T(1,128)}, u32[]{:S(2)}) copy-start(s32[1,16]{1,0:T(1,128)} %param.12) | copy-start | bytes 196
  9.4 41.0 %all-to-all-start = ((bf16[8,192,448]{2,1,0:T(8,128)(2,1)}), bf16[8,192,448]{2,1,0:T(8,128)(2,1)S(1)}, u32[]{:S(2)}, u32[]{:S(2)}) async-start(bf16[8,192,448]{2,1,0:T(8,128)(2,1)} %stack.30), calls=%async_computation | async-start | bytes 3145728 | tf_op jit(solution)/shard_map/all_to_all | solution.py:40
  20.7 83.5 %all-gather.6.cloned.1.call-start = ((), (), s32[]{:S(2)}) async-start(), calls=%async_computation.4 | async-start | bytes 1769472 | tf_op jit(solution)/shard_map/all_gather | solution.py:42
  21.4 193.5 %all-gather.4.cloned.1.call-start = ((), (), s32[]{:S(2)}) async-start(), calls=%async_computation.3 | async-start | bytes 3981312 | tf_op jit(solution)/shard_map/all_gather | solution.py:74
  109.1 2.9 copy-start
  118.5 0.7 copy-start.1
  122.3 2.7 copy-start.2
  122.3 210.7 %reduce-scatter.7.cloned.1.call-start = ((), (), s32[]{:S(2)}) async-start(), calls=%async_computation.5 | async-start | bytes 4128768
  134.1 350.2 %reduce-scatter.9.cloned.1.call-start = ((), (), s32[]{:S(2)}) async-start(), calls=%async_computation.6 | async-start | bytes 5677056
  226.1 258.2 %copy-start.3 = (f32[3,8,3584]{2,1,0:T(8,128)S(1)}, f32[3,8,3584]{2,1,0:T(8,128)}, u32[]{:S(2)}) copy-start(f32[3,8,3584]{2,1,0:T(8,128)} %param.13) | copy-start | bytes 1032196
  226.1 258.2 %copy-start.4 = (f32[3,8,3584]{2,1,0:T(8,128)S(1)}, f32[3,8,3584]{2,1,0:T(8,128)}, u32[]{:S(2)}) copy-start(f32[3,8,3584]{2,1,0:T(8,128)} %param.14) | copy-start | bytes 1032196
  226.1 258.2 %copy-start.5 = (f32[3,8,3584]{2,1,0:T(8,128)S(1)}, f32[3,8,3584]{2,1,0:T(8,128)}, u32[]{:S(2)}) copy-start(f32[3,8,3584]{2,1,0:T(8,128)} %param.15) | copy-start | bytes 1032196
Sparse Core Ops, SparseCore 0:
  24.1 79.9 all-gather.5
  122.4 92.4 all-gather.3
  219.2 113.7 reduce-scatter.6
  335.6 148.6 reduce-scatter.8
